TPU v7x, 32 devices: a whole 2x2x4 slice. The times are simulated.
32 devices in a mesh: groups: 2 (over y), dp: 4 (over z), mp: 2 (over x), seq: 2 (over core).
Axes of the slice: x: 2, y: 2, z: 4, core: 2. Of those that a mesh axis runs over, the one named last changes fastest.
Arguments:
- hidden: bfloat16 [32, 128, 14336], P(('groups', 'dp', 'seq'), None, 'mp'), parts along dimension 0, may hold values from -6 to 6
- down_weight: bfloat16 [14336, 4096], P('mp', 'dp'), may hold values from -0.046875 to 0.046875
- residual: bfloat16 [32, 128, 4096], P(('groups', 'dp', 'seq'), None, 'mp'), parts along dimension 0
- norm_gain: float32 [4096], P('mp'), may hold values from 0.5 to 1.5
- lengths: int32 [32], P(('groups', 'dp', 'seq')), parts along dimension 0, may hold values from 16 to 128
- queries: bfloat16 [8, 4096], P(('groups', 'dp'), 'mp'), parts along dimension 0
- positive_ids: int32 [8], P(('groups', 'dp')), parts along dimension 0, may hold values from 0 to 15
- negative_ids: int32 [8, 31], P(('groups', 'dp')), parts along dimension 0, may hold values from 0 to 15, as said below
- rerank_scores: int32 [8, 32], P(('groups', 'dp')), parts along dimension 0, may hold values from -64 to 63
Outputs:
- normed: bfloat16 [32, 128, 4096], P(('groups', 'dp', 'seq'), None, 'mp'), parts along dimension 0
- similarity_matrix: float32 [8, 32], P(('groups', 'dp')), parts along dimension 0
- losses: float32 [8], P(('groups', 'dp')), parts along dimension 0
There are 2 independent parts, one for each index of `groups`. A program takes and returns all parts, laid end to end along the dimension named above; an argument that names none is the same for every part. Nothing has to cross between parts.
Inputs may be any that keep to these rules, and one draw needn't show every extreme that they name: `negative_ids`: no hard negative of a query lies among the 4 passages with the query's own index of dp; the query with index q has dp index q, and the passage with index p has dp index p // 4.
All inputs are finite; a program needn't handle non-finite values.
Results may differ from a plain program's by a relative error of at most 0.001.
Values may be sent and summed in bfloat16 or wider, within the bound.
A program may use at most 192 MiB of HBM per device.

v0:
```python
import jax
import jax.numpy as jnp
from jax import lax
from jax.sharding import PartitionSpec as P

D = 4096


epsilon = 1e-05
safety_margin = 1e-06
sharpness_divisor = 0.05
teacher_scale = 8.0


def partition_logarithm(value_rows):
    return jnp.log(jnp.sum(jnp.exp(value_rows), axis=-1, keepdims=True))


def local(
    hidden,
    down_weight,
    residual,
    norm_gain,
    lengths,
    queries,
    positive_ids,
    negative_ids,
    rerank_scores,
):
    passages, tok_len, hidden_width = hidden.shape
    flattened = hidden.reshape(passages * tok_len, hidden_width)
    partial_sum = jnp.dot(
        flattened,
        lax.all_gather(down_weight, "dp", axis=1, tiled=True),
        preferred_element_type=jnp.float32,
    )
    partial_sum = partial_sum.reshape(passages, tok_len, D)
    branch_sum = lax.psum_scatter(partial_sum, "mp", scatter_dimension=2, tiled=True)
    updated = residual.astype(jnp.float32) + branch_sum
    squares = lax.psum(jnp.sum(updated * updated, axis=-1), "mp")
    unit_rows = updated * lax.rsqrt(squares / D + epsilon)[:, :, None]
    scaled = unit_rows * norm_gain[None, None, :]
    position = jnp.arange(tok_len, dtype=jnp.int32)
    valid_mask = position[None, :] < lengths[:, None]
    pooled_share = (
        jnp.sum(jnp.where(valid_mask[:, :, None], scaled, 0.0), axis=1)
        / lengths.astype(jnp.float32)[:, None]
    )
    averaged_embedding = lax.all_gather(pooled_share, ("dp", "seq"), axis=0, tiled=True)
    total_passages = averaged_embedding.shape[0]
    candidates = jnp.concatenate([positive_ids[:, None], negative_ids], axis=1)
    one_hot = (
        candidates[:, :, None] == jnp.arange(total_passages, dtype=jnp.int32)[None, None, :]
    ).astype(jnp.float32)
    picked = jnp.einsum("qcp,pd->qcd", one_hot, averaged_embedding, precision=lax.Precision.HIGHEST)
    query_vals = queries.astype(jnp.float32)
    cosine_numerator = jnp.einsum("qd,qcd->qc", query_vals, picked, precision=lax.Precision.HIGHEST)
    candidate_length_power = jnp.sum(picked * picked, axis=-1)
    question_length_power = jnp.sum(query_vals * query_vals, axis=-1)
    cosine_numerator, candidate_length_power, question_length_power = lax.psum(
        (cosine_numerator, candidate_length_power, question_length_power), "mp"
    )
    similarity_matrix = (
        cosine_numerator
        * lax.rsqrt(question_length_power + safety_margin)[:, None]
        * lax.rsqrt(candidate_length_power + safety_margin)
        / sharpness_divisor
    )
    log_student = similarity_matrix - partition_logarithm(similarity_matrix)
    teacher = rerank_scores.astype(jnp.float32) / teacher_scale
    teacher_log_probs = teacher - partition_logarithm(teacher)
    losses = -log_student[:, 0] + jnp.sum(
        jnp.exp(teacher_log_probs) * (teacher_log_probs - log_student), axis=-1
    )
    return (scaled.astype(jnp.bfloat16), similarity_matrix, losses)


def solution(mesh):
    return jax.shard_map(
        local,
        mesh=mesh,
        in_specs=(
            P(("groups", "dp", "seq"), None, "mp"),
            P("mp", "dp"),
            P(("groups", "dp", "seq"), None, "mp"),
            P("mp"),
            P(("groups", "dp", "seq")),
            P(("groups", "dp"), "mp"),
            P(("groups", "dp")),
            P(("groups", "dp"), None),
            P(("groups", "dp"), None),
        ),
        out_specs=(
            P(("groups", "dp", "seq"), None, "mp"),
            P(("groups", "dp"), None),
            P(("groups", "dp")),
        ),
        check_vma=False,
    )
```

profile of v0, /device:TPU:0, one launch (start us, length us, event | category | flops | bytes accessed | tf_op | source)
XLA Modules:
  0.0 1105.5 jit_solution(8888944107291363189)
XLA Ops:
  7.2 0.0 all-gather.3.cloned.1.call-start
  7.2 0.7 all-gather.3.cloned.1.call-update
  7.9 0.0 reduce-scatter.2.cloned.1.call-start
  7.9 978.8 %all-gather.3.cloned.1.call-done = bf16[7168,4096]{1,0:T(8,128)(2,1)} async-done(((bf16[7168,1024]{1,0:T(8,128)(2,1)}), bf16[7168,4096]{1,0:T(8,128)(2,1)}) %all-gather.3.cloned.1.call-update) | async-done | bytes 58720272 | tf_op jit(solution)/shard_map/all_gather | solution.py:34
  986.7 25.6 %fusion = f32[2,128,4096]{2,1,0:T(8,128)} fusion(bf16[2,128,7168]{2,1,0:T(8,128)(2,1)} %param.9, bf16[7168,4096]{1,0:T(8,128)(2,1)} %all-gather.3.cloned.1.call-done), kind=kOutput, calls=%fused_computation | convolution fusion | flops 15032385536 | bytes 66584576 | tf_op jit(solution)/shard_map/dot_general | solution.py:32
  1012.3 0.0 copy-start.2
  1012.3 0.0 copy-start.1
  1012.3 0.0 reduce-scatter.2.cloned.1.call-update
  1012.4 0.6 copy-done.7
  1013.6 0.0 copy-done.5
  1013.6 0.6 exponential_reduce_fusion
  1014.9 0.0 copy-done.6
  1015.0 0.1 add_bitcast_fusion
  1015.0 0.0 copy-done.2
  1015.0 0.6 multiply_reduce_fusion.2
  1015.6 0.1 iota_compare_fusion.2
  1015.7 49.3 %reduce-scatter.2.cloned.1.call-done = f32[2,128,2048]{2,1,0:T(8,128)} async-done(((f32[2,128,4096]{2,1,0:T(8,128)}), f32[2,128,2048]{2,1,0:T(8,128)}) %reduce-scatter.2.cloned.1.call-update) | async-done | bytes 2097168 | tf_op jit(solution)/shard_map/reduce_scatter | solution.py:38
  1065.0 0.0 copy-done.1
  1065.0 2.1 multiply_reduce_fusion
  1067.1 4.9 psum.28
  1072.1 0.0 copy-done.3
  1072.1 0.0 copy-done
  1072.1 1.5 select_reduce_fusion
  1073.6 0.1 divide_bitcast_fusion
  1073.7 14.1 %all-gather = f32[8,2,2048]{2,1,0:T(2,128)S(1)} all-gather(f32[1,2,2048]{2,1,0:T(2,128)S(1)} %divide_bitcast_fusion), channel_id=1, replica_groups=mesh['groups'=2,'dp'=4,'mp'=2,'seq'=2] {'dp','seq'}, dimensions={0}, use_global_device_ids=true | all-gather | bytes 147456 | tf_op jit(solution)/shard_map/all_gather | solution.py:49
  1087.7 0.1 reshape.81
  1087.8 0.4 multiply_reduce_fusion.1
  1088.2 0.2 fusion.4
  1088.4 5.6 all-reduce
  1094.7 0.7 exponential_reduce_fusion.1
  1096.2 0.6 multiply_reduce_fusion.3
  1097.5 0.0 copy-done.4
  (8 shorter events, 0.0 us)
Async XLA Ops:
  7.2 979.6 %all-gather.3.cloned.1.call-start = ((), (), s32[]{:S(2)}) async-start(), calls=%async_computation.1 | async-start | bytes 73400320 | tf_op jit(solution)/shard_map/all_gather | solution.py:34
  7.9 1057.1 %reduce-scatter.2.cloned.1.call-start = ((), (), s32[]{:S(2)}) async-start(), calls=%async_computation.2 | async-start | bytes 6291456 | tf_op jit(solution)/shard_map/reduce_scatter | solution.py:38
  1012.3 0.7 copy-start.7
  1012.3 1.3 copy-start.5
  1012.3 2.6 copy-start.6
  1012.3 2.7 copy-start.2
  1012.3 52.7 %copy-start.1 = (bf16[2,128,2048]{2,1,0:T(8,128)(2,1)S(1)}, bf16[2,128,2048]{2,1,0:T(8,128)(2,1)}, u32[]{:S(2)}) copy-start(bf16[2,128,2048]{2,1,0:T(8,128)(2,1)} %param.11) | copy-start | bytes 3145732
  1013.0 59.1 %copy-start.3 = (f32[2048]{0:T(1024)S(1)}, f32[2048]{0:T(1024)}, u32[]{:S(2)}) copy-start(f32[2048]{0:T(1024)} %param.12) | copy-start | bytes 24580
  1065.0 7.1 copy-start
  1095.4 2.0 copy-start.4
Sparse Core Ops, SparseCore 0:
  9.6 977.0 all-gather.2
  1012.5 52.4 reduce-scatter.1
where the time goes:
time: 1110 us
  waiting for transfers between devices  1030 us (93%)
  matrix products  26.2 us (2%)
  blocking collectives  24.6 us (2%)
  between operations  18.7 us (2%)
    all_gather x1, waiting for transfers between devices, local(): lax.all_gather(down_weight, 'dp', axis=1, tiled=True)  979 us
    reduce_scatter x1, waiting for transfers between devices, local(): lax.psum_scatter(partial_sum, 'mp', scatter_dimension=2, tiled=True)  49.3 us
    dot_general x1, matrix products, local(): jnp.dot(flattened, lax.all_gather(down_weight, 'dp', axis=1, tiled=True),...  25.6 us
  transfers between devices with their start and end apart: 2, of which 2 were waited for; matrix products, arithmetic and copies ran while one was open for 0% of the time, Pallas kernels for 0%

commit v1 on v0

--- a/solution.py
+++ b/solution.py
@@ -1,6 +1,10 @@
+import functools
+
 import jax
 import jax.numpy as jnp
 from jax import lax
+from jax.experimental import pallas as pl
+from jax.experimental.pallas import tpu as pltpu
 from jax.sharding import PartitionSpec as P
 
 D = 4096
@@ -16,7 +20,145 @@
     return jnp.log(jnp.sum(jnp.exp(value_rows), axis=-1, keepdims=True))
 
 
+MESH = pl.DeviceIdType.MESH
+CHUNKS = 7
+RIGHT, LEFT, ACROSS, CORE, CORE_ACROSS = range(5)
+
+
+def gather_kernel(n, w_ref, o_ref, own_sem, send, recv):
+    z = lax.axis_index("dp")
+    y = lax.axis_index("groups")
+    c = lax.axis_index("seq")
+    depth, cols = w_ref.shape
+    quarter = depth // 4
+    size = quarter // CHUNKS
+    mine = y * 2 + c
+    other = (1 - y) * 2 + c
+    to = {
+        RIGHT: {"dp": jnp.minimum(z + 1, n - 1)},
+        LEFT: {"dp": jnp.maximum(z - 1, 0)},
+        ACROSS: {"groups": 1 - y},
+        CORE: {"seq": 1 - c},
+        CORE_ACROSS: {"seq": 1 - c},
+    }
+
+    barrier = pltpu.get_barrier_semaphore()
+    pl.semaphore_signal(barrier, inc=1, device_id=to[ACROSS], device_id_type=MESH)
+    pl.semaphore_signal(barrier, inc=1, device_id=to[CORE], device_id_type=MESH)
+
+    @pl.when(z < n - 1)
+    def _():
+        pl.semaphore_signal(barrier, inc=1, device_id=to[RIGHT], device_id_type=MESH)
+
+    @pl.when(z > 0)
+    def _():
+        pl.semaphore_signal(barrier, inc=1, device_id=to[LEFT], device_id_type=MESH)
+
+    own_cols = pl.ds(pl.multiple_of(z * cols, 128), cols)
+    own = pltpu.make_async_copy(w_ref, o_ref.at[:, own_cols], own_sem)
+    own.start()
+    peers = 2 + (z < n - 1).astype(jnp.int32) + (z > 0).astype(jnp.int32)
+    pl.semaphore_wait(barrier, peers)
+
+    def rows(q, k):
+        return pl.ds(pl.multiple_of(q * quarter + k * size, 16), size)
+
+    def copy(kind, b, q, k, own_source=False):
+        place = o_ref.at[rows(q, k), pl.ds(pl.multiple_of(b * cols, 128), cols)]
+        return pltpu.make_async_remote_copy(
+            src_ref=w_ref.at[rows(q, k), :] if own_source else place,
+            dst_ref=place,
+            send_sem=send.at[kind, b, k],
+            recv_sem=recv.at[kind, b, k],
+            device_id=to[kind],
+            device_id_type=MESH,
+        )
+
+    def exists(sign, j):
+        b = z + sign * j
+        return jnp.logical_and(b >= 0, b < n)
+
+    def stream(kind, sign, t):
+        j, k = t // CHUNKS, t % CHUNKS
+        b = z + sign * j
+        goes_on = (z < n - 1) if kind == RIGHT else (z > 0)
+
+        @pl.when(jnp.logical_and(j == 0, goes_on))
+        def _():
+            copy(kind, z, mine, k, own_source=True).start()
+
+        @pl.when(jnp.logical_and(jnp.logical_and(j >= 1, j < n), exists(sign, j)))
+        def _():
+            copy(kind, b, mine, k).wait_recv()
+
+            @pl.when(goes_on)
+            def _():
+                copy(kind, b, mine, k).start()
+
+            copy(ACROSS, b, mine, k).start()
+            copy(CORE, b, mine, k).start()
+
+        before = t - 2
+        jb, kb = before // CHUNKS, before % CHUNKS
+
+        @pl.when(jnp.logical_and(jnp.logical_and(before >= 0, goes_on), exists(sign, jb)))
+        def _():
+            copy(kind, z + sign * jb, mine, kb).wait_send()
+
+    def crossed(sign, t):
+        j, k = t // CHUNKS, t % CHUNKS
+        b = z + sign * j
+
+        @pl.when(jnp.logical_and(jnp.logical_and(j >= 1, j < n), exists(sign, j)))
+        def _():
+            copy(ACROSS, b, other, k).wait_recv()
+            copy(CORE_ACROSS, b, other, k).start()
+
+    def step(t, carry):
+        stream(RIGHT, -1, t)
+        stream(LEFT, 1, t)
+        crossed(-1, t - 1)
+        crossed(1, t - 1)
+        return carry
+
+    lax.fori_loop(0, n * CHUNKS + 2, step, 0)
+
+    def drain(t, carry):
+        b, k = t // CHUNKS, t % CHUNKS
+
+        @pl.when(b != z)
+        def _():
+            copy(ACROSS, b, mine, k).wait_send()
+            copy(CORE, b, mine, k).wait()
+            copy(CORE_ACROSS, b, other, k).wait()
+
+        return carry
+
+    lax.fori_loop(0, n * CHUNKS, drain, 0)
+    own.wait()
+
+
+def gather_weight(n, weight):
+    depth, cols = weight.shape
+    return pl.pallas_call(
+        functools.partial(gather_kernel, n),
+        out_shape=jax.ShapeDtypeStruct((depth, n * cols), weight.dtype),
+        in_specs=[pl.BlockSpec(memory_space=pl.ANY)],
+        out_specs=pl.BlockSpec(memory_space=pl.ANY),
+        scratch_shapes=[
+            pltpu.SemaphoreType.DMA,
+            pltpu.SemaphoreType.DMA((5, n, CHUNKS)),
+            pltpu.SemaphoreType.DMA((5, n, CHUNKS)),
+        ],
+        compiler_params=pltpu.CompilerParams(collective_id=0, has_side_effects=True),
+        cost_estimate=pl.CostEstimate(
+            flops=0, bytes_accessed=4 * n * depth * cols, transcendentals=0
+        ),
+    )(weight)
+
+
 def local(
+    n,
     hidden,
     down_weight,
     residual,
@@ -31,7 +173,7 @@
     flattened = hidden.reshape(passages * tok_len, hidden_width)
     partial_sum = jnp.dot(
         flattened,
-        lax.all_gather(down_weight, "dp", axis=1, tiled=True),
+        gather_weight(n, down_weight),
         preferred_element_type=jnp.float32,
     )
     partial_sum = partial_sum.reshape(passages, tok_len, D)
@@ -77,7 +219,7 @@
 
 def solution(mesh):
     return jax.shard_map(
-        local,
+        functools.partial(local, mesh.shape["dp"]),
         mesh=mesh,
         in_specs=(
             P(("groups", "dp", "seq"), None, "mp"),

time: 1110 us -> 579 us (0.52)
  waiting for transfers between devices: 1030 us -> 53.8 us
  Pallas kernels: 0 us -> 448 us
    all_gather x1 -> x0, waiting for transfers between devices: 979 us -> none  [local(): lax.all_gather(down_weight, 'dp', axis=1, tiled=True)]
    pallas_call x0 -> x1, Pallas kernels: none -> 448 us  [gather_weight(): pl.pallas_call(functools.partial(gather_kernel, n), out_shape=jax.ShapeDt...]
  transfers between devices with their start and end apart: 2 -> 1, of which waited for: 2 -> 1; matrix products, arithmetic and copies ran while one was open for 0% -> 0% of each run, Pallas kernels for 0% -> 0%
where the time goes in v1:
time: 579 us
  Pallas kernels  448 us (77%)
  waiting for transfers between devices  53.8 us (9%)
  matrix products  26.2 us (5%)
  blocking collectives  24.6 us (4%)
  between operations  18.7 us (3%)
  other arithmetic  6.4 us (1%)
    pallas_call x1, Pallas kernels, gather_weight(): pl.pallas_call(functools.partial(gather_kernel, n), out_shape=jax.ShapeDt...  448 us
    reduce_scatter x1, waiting for transfers between devices, local(): lax.psum_scatter(partial_sum, 'mp', scatter_dimension=2, tiled=True)  53.8 us
    dot_general x1, matrix products, local(): jnp.dot(flattened, gather_weight(n, down_weight), preferred_element_type=...  25.6 us
    all_gather x1, blocking collectives, local(): lax.all_gather(pooled_share, ('dp', 'seq'), axis=0, tiled=True)  14.1 us
  transfers between devices with their start and end apart: 1, of which 1 were waited for; matrix products, arithmetic and copies ran while one was open for 0% of the time, Pallas kernels for 0%

profile of v1, /device:TPU:0, one launch (start us, length us, event | category | flops | bytes accessed | tf_op | source)
XLA Modules:
  0.0 578.9 jit_solution(16068100348133567767)
XLA Ops:
  7.2 0.0 reduce-scatter.2.cloned.1.call-start
  7.2 448.4 %shard_map.112 = bf16[7168,4096]{1,0:T(8,128)(2,1)} custom-call(bf16[7168,1024]{1,0:T(8,128)(2,1)} %w_ref.1), custom_call_target="tpu_custom_call" | custom-call | bytes 117440512 | tf_op jit(solution)/shard_map/pallas_call | solution.py:143
  455.6 25.6 %fusion = f32[2,128,4096]{2,1,0:T(8,128)} fusion(bf16[2,128,7168]{2,1,0:T(8,128)(2,1)} %param.9, bf16[7168,4096]{1,0:T(8,128)(2,1)} %shard_map.112), kind=kOutput, calls=%fused_computation | convolution fusion | flops 15032385536 | bytes 66584576 | tf_op jit(solution)/shard_map/dot_general | solution.py:174
  481.2 0.0 copy-start.7
  481.2 0.0 copy-start.5
  481.2 0.0 copy-start.2
  481.2 0.0 copy-start.1
  481.2 0.0 reduce-scatter.2.cloned.1.call-update
  481.3 0.6 copy-done.7
  482.5 0.0 copy-done.5
  482.5 0.6 exponential_reduce_fusion
  483.8 0.0 copy-done.6
  483.9 0.1 add_bitcast_fusion
  483.9 0.0 copy-done.2
  483.9 0.6 multiply_reduce_fusion.2
  484.5 0.1 iota_compare_fusion.2
  484.6 53.8 %reduce-scatter.2.cloned.1.call-done = f32[2,128,2048]{2,1,0:T(8,128)} async-done(((f32[2,128,4096]{2,1,0:T(8,128)}), f32[2,128,2048]{2,1,0:T(8,128)}) %reduce-scatter.2.cloned.1.call-update) | async-done | bytes 2097168 | tf_op jit(solution)/shard_map/reduce_scatter | solution.py:180
  538.4 0.0 copy-done.1
  538.4 2.1 multiply_reduce_fusion
  540.5 4.9 psum.28
  545.5 0.0 copy-done.3
  545.5 0.0 copy-done
  545.5 1.5 select_reduce_fusion
  547.0 0.1 divide_bitcast_fusion
  547.1 14.1 %all-gather = f32[8,2,2048]{2,1,0:T(2,128)S(1)} all-gather(f32[1,2,2048]{2,1,0:T(2,128)S(1)} %divide_bitcast_fusion), channel_id=1, replica_groups=mesh['groups'=2,'dp'=4,'mp'=2,'seq'=2] {'dp','seq'}, dimensions={0}, use_global_device_ids=true | all-gather | bytes 147456 | tf_op jit(solution)/shard_map/all_gather | solution.py:191
  561.2 0.1 reshape.81
  561.2 0.4 multiply_reduce_fusion.1
  561.7 0.2 fusion.4
  561.9 5.6 all-reduce
  568.2 0.7 exponential_reduce_fusion.1
  569.6 0.6 multiply_reduce_fusion.3
  570.9 0.0 copy-done.4
  (6 shorter events, 0.0 us)
Async XLA Ops:
  7.2 531.2 %reduce-scatter.2.cloned.1.call-start = ((), (), s32[]{:S(2)}) async-start(), calls=%async_computation.1 | async-start | bytes 6291456 | tf_op jit(solution)/shard_map/reduce_scatter | solution.py:180
  481.2 0.7 copy-start.7
  481.2 1.3 copy-start.5
  481.2 2.6 copy-start.6
  481.2 2.7 copy-start.2
  481.2 57.2 %copy-start.1 = (bf16[2,128,2048]{2,1,0:T(8,128)(2,1)S(1)}, bf16[2,128,2048]{2,1,0:T(8,128)(2,1)}, u32[]{:S(2)}) copy-start(bf16[2,128,2048]{2,1,0:T(8,128)(2,1)} %param.11) | copy-start | bytes 3145732
  481.9 63.6 %copy-start.3 = (f32[2048]{0:T(1024)S(1)}, f32[2048]{0:T(1024)}, u32[]{:S(2)}) copy-start(f32[2048]{0:T(1024)} %param.12) | copy-start | bytes 24580
  538.4 7.1 %copy-start = (f32[2,128,2048]{2,1,0:T(8,128)S(1)}, f32[2,128,2048]{2,1,0:T(8,128)}, u32[]{:S(2)}) copy-start(f32[2,128,2048]{2,1,0:T(8,128)} %reduce-scatter.2.cloned.1.call-done) | copy-start | bytes 6291460
  568.9 2.0 copy-start.4
Sparse Core Ops, SparseCore 0:
  481.4 56.9 reduce-scatter.1

commit v2 on v0

--- a/solution.py
+++ b/solution.py
@@ -1,6 +1,10 @@
+import functools
+
 import jax
 import jax.numpy as jnp
 from jax import lax
+from jax.experimental import pallas as pl
+from jax.experimental.pallas import tpu as pltpu
 from jax.sharding import PartitionSpec as P
 
 D = 4096
@@ -16,7 +20,212 @@
     return jnp.log(jnp.sum(jnp.exp(value_rows), axis=-1, keepdims=True))
 
 
+MESH = pl.DeviceIdType.MESH
+CHUNKS = 14
+WINDOW = 3
+LAG = 2
+RIGHT, LEFT, ACROSS, CORE, CORE_ACROSS = range(5)
+
+
+def both(*terms):
+    return functools.reduce(jnp.logical_and, terms)
+
+
+def gather_kernel(w_ref, h_ref, o_ref, p_ref, t_ref, own_sem, h_send, h_recv, send, recv):
+    z = lax.axis_index("dp")
+    y = lax.axis_index("groups")
+    c = lax.axis_index("seq")
+    depth = w_ref.shape[0]
+    quarter = depth // 4
+    size = quarter // CHUNKS
+    mine = y * 2 + c
+    other = (1 - y) * 2 + c
+    pair = z + 1 - 2 * (z % 2)
+    to = {
+        RIGHT: {"dp": jnp.minimum(z + 1, 3)},
+        LEFT: {"dp": jnp.maximum(z - 1, 0)},
+        ACROSS: {"groups": 1 - y},
+        CORE: {"seq": 1 - c},
+        CORE_ACROSS: {"seq": 1 - c},
+    }
+
+    barrier = pltpu.get_barrier_semaphore()
+    pl.semaphore_signal(barrier, inc=1, device_id=to[ACROSS], device_id_type=MESH)
+    pl.semaphore_signal(barrier, inc=1, device_id=to[CORE], device_id_type=MESH)
+
+    @pl.when(z < 3)
+    def _():
+        pl.semaphore_signal(barrier, inc=1, device_id=to[RIGHT], device_id_type=MESH)
+
+    @pl.when(z > 0)
+    def _():
+        pl.semaphore_signal(barrier, inc=1, device_id=to[LEFT], device_id_type=MESH)
+
+    peers = 2 + (z < 3).astype(jnp.int32) + (z > 0).astype(jnp.int32)
+    pl.semaphore_wait(barrier, peers)
+
+    def rows(q, k):
+        return pl.ds(pl.multiple_of(q * quarter + k * size, 16), size)
+
+    def part(k):
+        return pl.ds(pl.multiple_of(k * size, 16), size)
+
+    def remote(kind, j, k, src, dst, arrives):
+        return pltpu.make_async_remote_copy(
+            src_ref=src,
+            dst_ref=dst,
+            send_sem=send.at[kind, j, k],
+            recv_sem=recv.at[kind, arrives, k],
+            device_id=to[kind],
+            device_id_type=MESH,
+        )
+
+    def along(kind, j, k):
+        return remote(kind, j, k, p_ref.at[part(k), :], p_ref.at[part(k), :], j)
+
+    def shared(kind, j, k, q):
+        block = jnp.where(z >= 2, z - j, z + j) % 2
+        place = o_ref.at[block, rows(q, k), :]
+        return remote(kind, j, k, place, place, j)
+
+    def stream(kind, t):
+        u = z if kind == RIGHT else 3 - z
+        sign = -1 if kind == RIGHT else 1
+        j, k = t // CHUNKS, t % CHUNKS
+        own = w_ref.at[rows(mine, k), :]
+        passing = p_ref.at[part(k), :]
+
+        @pl.when(both(j == 0, u == 0))
+        def _():
+            remote(kind, 0, k, own, passing, 1).start()
+
+        @pl.when(both(j == 0, u >= 1, u <= 2))
+        def _():
+            remote(kind, 0, k, own, o_ref.at[z % 2, rows(mine, k), :], 1).start()
+
+        @pl.when(both(j == 1, u == 1))
+        def _():
+            along(kind, 1, k).wait_recv()
+            place = o_ref.at[(z + sign) % 2, rows(mine, k), :]
+            remote(kind, 1, k, passing, place, 2).start()
+
+        @pl.when(jnp.logical_or(both(j == 1, u >= 2), both(j == 2, u == 2)))
+        def _():
+            along(kind, j, k).wait_recv()
+            shared(ACROSS, j, k, mine).start()
+            shared(CORE, j, k, mine).start()
+
+        before = t - WINDOW
+        jb, kb = before // CHUNKS, before % CHUNKS
+        sent = jnp.logical_or(both(jb == 0, u <= 2), both(jb == 1, u == 1))
+
+        @pl.when(both(before >= 0, sent))
+        def _():
+            along(kind, jb, kb).wait_send()
+
+    def needed(j):
+        return jnp.logical_or(j == 1, both(j == 2, z >= 1, z <= 2))
+
+    swap = pltpu.make_async_remote_copy(
+        src_ref=h_ref,
+        dst_ref=t_ref,
+        send_sem=h_send,
+        recv_sem=h_recv,
+        device_id={"dp": pair},
+        device_id_type=MESH,
+    )
+    outer = jnp.logical_or(z == 0, z == 3)
+    keep = pltpu.make_async_copy(w_ref, o_ref.at[z % 2], own_sem)
+
+    def step(t, carry):
+        stream(RIGHT, t)
+        stream(LEFT, t)
+        late = t - LAG
+        j, k = late // CHUNKS, late % CHUNKS
+
+        @pl.when(both(late >= 0, needed(j)))
+        def _():
+            shared(ACROSS, j, k, other).wait_recv()
+            shared(CORE_ACROSS, j, k, other).start()
+
+        @pl.when(t == CHUNKS)
+        def _():
+            swap.start()
+
+            @pl.when(outer)
+            def _():
+                keep.start()
+
+        return carry
+
+    lax.fori_loop(0, 3 * CHUNKS + max(WINDOW, LAG), step, 0)
+
+    def drain(t, carry):
+        j, k = t // CHUNKS, t % CHUNKS
+
+        @pl.when(needed(j))
+        def _():
+            shared(ACROSS, j, k, mine).wait_send()
+            shared(CORE, j, k, mine).wait_send()
+            shared(CORE, j, k, y * 2 + 1 - c).wait_recv()
+            shared(CORE_ACROSS, j, k, other).wait_send()
+            shared(CORE_ACROSS, j, k, (1 - y) * 2 + 1 - c).wait_recv()
+
+        return carry
+
+    lax.fori_loop(CHUNKS, 3 * CHUNKS, drain, 0)
+    swap.wait()
+
+    @pl.when(outer)
+    def _():
+        keep.wait()
+
+
+def gather(weight, rows):
+    depth, cols = weight.shape
+    return pl.pallas_call(
+        gather_kernel,
+        out_shape=(
+            jax.ShapeDtypeStruct((2, depth, cols), weight.dtype),
+            jax.ShapeDtypeStruct((depth // 4, cols), weight.dtype),
+            jax.ShapeDtypeStruct(rows.shape, rows.dtype),
+        ),
+        in_specs=[pl.BlockSpec(memory_space=pl.ANY)] * 2,
+        out_specs=(pl.BlockSpec(memory_space=pl.ANY),) * 3,
+        scratch_shapes=[
+            pltpu.SemaphoreType.DMA,
+            pltpu.SemaphoreType.DMA,
+            pltpu.SemaphoreType.DMA,
+            pltpu.SemaphoreType.DMA((5, 3, CHUNKS)),
+            pltpu.SemaphoreType.DMA((5, 3, CHUNKS)),
+        ],
+        compiler_params=pltpu.CompilerParams(collective_id=0, has_side_effects=True),
+        cost_estimate=pl.CostEstimate(
+            flops=0, bytes_accessed=16 * depth * cols, transcendentals=0
+        ),
+    )(weight, rows)
+
+
+def paired_branch(flattened, weight):
+    blocks, _, theirs = gather(weight, flattened)
+    half = lax.axis_index("dp") % 2
+    kept_here = half == lax.axis_index("mp")
+    swap_pair = [(z, z + 1 - 2 * (z % 2)) for z in range(4)]
+    sums = []
+    back = []
+    for s in range(2):
+        away = jnp.dot(theirs, blocks[s], preferred_element_type=jnp.float32)
+        back.append(lax.ppermute(away, "dp", swap_pair))
+    for s in range(2):
+        own = jnp.dot(flattened, blocks[s], preferred_element_type=jnp.float32)
+        leaves = jnp.where(kept_here, back[s], own)
+        stays = jnp.where(kept_here, own, back[s])
+        sums.append(stays + lax.ppermute(leaves, "mp", [(0, 1), (1, 0)]))
+    return jnp.concatenate(sums, axis=1)
+
+
 def local(
+    paired,
     hidden,
     down_weight,
     residual,
@@ -29,13 +238,16 @@
 ):
     passages, tok_len, hidden_width = hidden.shape
     flattened = hidden.reshape(passages * tok_len, hidden_width)
-    partial_sum = jnp.dot(
-        flattened,
-        lax.all_gather(down_weight, "dp", axis=1, tiled=True),
-        preferred_element_type=jnp.float32,
-    )
-    partial_sum = partial_sum.reshape(passages, tok_len, D)
-    branch_sum = lax.psum_scatter(partial_sum, "mp", scatter_dimension=2, tiled=True)
+    if paired:
+        branch_sum = paired_branch(flattened, down_weight).reshape(residual.shape)
+    else:
+        partial_sum = jnp.dot(
+            flattened,
+            lax.all_gather(down_weight, "dp", axis=1, tiled=True),
+            preferred_element_type=jnp.float32,
+        )
+        partial_sum = partial_sum.reshape(passages, tok_len, D)
+        branch_sum = lax.psum_scatter(partial_sum, "mp", scatter_dimension=2, tiled=True)
     updated = residual.astype(jnp.float32) + branch_sum
     squares = lax.psum(jnp.sum(updated * updated, axis=-1), "mp")
     unit_rows = updated * lax.rsqrt(squares / D + epsilon)[:, :, None]
@@ -76,8 +288,10 @@
 
 
 def solution(mesh):
+    paired = (mesh.shape["dp"], mesh.shape["mp"]) == (4, 2)
+    paired = paired and (mesh.shape["groups"], mesh.shape["seq"]) == (2, 2)
     return jax.shard_map(
-        local,
+        functools.partial(local, paired),
         mesh=mesh,
         in_specs=(
             P(("groups", "dp", "seq"), None, "mp"),

time: 1110 us -> 649 us (0.58)
  waiting for transfers between devices: 1030 us -> 34.6 us
  Pallas kernels: 0 us -> 522 us
  matrix products: 26.2 us -> 45.9 us
  between operations: 18.7 us -> 5.34 us
    all_gather x1 -> x0, waiting for transfers between devices: 979 us -> none  [local(): lax.all_gather(down_weight, 'dp', axis=1, tiled=True)]
    pallas_call x0 -> x1, Pallas kernels: none -> 522 us  [gather(): pl.pallas_call(gather_kernel, out_shape=(jax.ShapeDtypeStruct((2, depth,...]
    reduce_scatter x1 -> x0, waiting for transfers between devices: 49.3 us -> none  [local(): lax.psum_scatter(partial_sum, 'mp', scatter_dimension=2, tiled=True)]
    ppermute x0 -> x4, waiting for transfers between devices: none -> 34.6 us  [the longest x2 17.5 us: paired_branch(): back.append(lax.ppermute(away, 'dp', swap_pair))]
    dot_general x1 -> x4, matrix products: 25.6 us -> 45.3 us  [the longest x2 23.4 us: paired_branch(): away = jnp.dot(theirs, blocks[s], preferred_element_type=jnp.float32)]
  transfers between devices with their start and end apart: 2 -> 4, of which waited for: 2 -> 3; matrix products, arithmetic and copies ran while one was open for 0% -> 6% of each run, Pallas kernels for 0% -> 0%
where the time goes in v2:
time: 649 us; the launch traced here: 648 us
  Pallas kernels  522 us (80%)
  matrix products  45.9 us (7%)
  waiting for transfers between devices  34.6 us (5%)
  blocking collectives  24.8 us (4%)
  other arithmetic  8.96 us (1%)
    pallas_call x1, Pallas kernels, gather(): pl.pallas_call(gather_kernel, out_shape=(jax.ShapeDtypeStruct((2, depth,...  522 us
    dot_general x2, matrix products, paired_branch(): away = jnp.dot(theirs, blocks[s], preferred_element_type=jnp.float32)  23.4 us
    dot_general x2, matrix products, paired_branch(): own = jnp.dot(flattened, blocks[s], preferred_element_type=jnp.float32)  21.9 us
    ppermute x2, waiting for transfers between devices, paired_branch(): back.append(lax.ppermute(away, 'dp', swap_pair))  17.5 us
    ppermute x2, waiting for transfers between devices, paired_branch(): sums.append(stays + lax.ppermute(leaves, 'mp', [(0, 1), (1, 0)]))  17.1 us
    all_gather x1, blocking collectives, local(): lax.all_gather(pooled_share, ('dp', 'seq'), axis=0, tiled=True)  14.2 us
  transfers between devices with their start and end apart: 4, of which 3 were waited for; matrix products, arithmetic and copies ran while one was open for 6% of the time, Pallas kernels for 0%

profile of v2, /device:TPU:0, one launch (start us, length us, event | category | flops | bytes accessed | tf_op | source)
XLA Modules:
  0.0 648.3 jit_solution(2979669034990280700)
XLA Ops:
  0.6 521.5 %shard_map.112 = (bf16[2,7168,1024]{2,1,0:T(8,128)(2,1)}, bf16[1792,1024]{1,0:T(8,128)(2,1)}, bf16[256,7168]{1,0:T(8,128)(2,1)}) custom-call(bf16[7168,1024]{1,0:T(8,128)(2,1)} %w_ref.1, bf16[256,7168]{1,0:T(8,128)(2,1)} %bitcast.49), custom_call_target="tpu_custom_call" | custom-call | bytes 117440512 | tf_op jit(solution)/shard_map/pallas_call | solution.py:186
  522.1 10.3 %fusion = f32[256,1024]{0,1:T(8,128)S(1)} fusion(bf16[256,7168]{1,0:T(8,128)(2,1)} %get-tuple-element.6, bf16[2,7168,1024]{2,1,0:T(8,128)(2,1)} %get-tuple-element.5), kind=kOutput, calls=%fused_computation | convolution fusion | flops 3758096384 | bytes 19398656 | tf_op jit(solution)/shard_map/dot_general | solution.py:217
  532.5 0.1 collective-permute-start.2
  532.5 13.1 %fusion.4 = f32[256,1024]{0,1:T(8,128)} fusion(bf16[256,7168]{1,0:T(8,128)(2,1)} %get-tuple-element.6, bf16[2,7168,1024]{2,1,0:T(8,128)(2,1)} %get-tuple-element.5), kind=kOutput, calls=%fused_computation.4 | convolution fusion | flops 3758096384 | bytes 19398656 | tf_op jit(solution)/shard_map/dot_general | solution.py:217
  545.6 2.0 collective-permute-start
  547.6 11.0 %collective-permute-done.2 = f32[256,1024]{0,1:T(8,128)S(1)} collective-permute-done((f32[256,1024]{0,1:T(8,128)S(1)}, f32[256,1024]{0,1:T(8,128)S(1)}, u32[]{:S(2)}, u32[]{:S(2)}) %collective-permute-start.2) | collective-permute-done | bytes 1048608 | tf_op jit(solution)/shard_map/ppermute | solution.py:218
  558.6 11.2 %broadcast_select_fusion = (f32[256,1024]{0,1:T(8,128)}, f32[256,1024]{0,1:T(8,128)S(1)}) fusion(f32[256,1024]{0,1:T(8,128)S(1)} %collective-permute-done.2, pred[]{:T(512)S(6)} %eq.23, bf16[256,7168]{1,0:T(8,128)(2,1)} %bitcast.50, bf16[2,7168,1024]{2,1,0:T(8,128)(2,1)} %get-tuple-element.5), kind=kOutput, calls=%fused_computation.22 | convolution fusion | flops 3758358528 | bytes 21495808 | tf_op jit(solution)/shard_map/dot_general | solution.py:220
  569.8 1.6 collective-permute-start.3
  571.4 6.5 %collective-permute-done = f32[256,1024]{0,1:T(8,128)S(1)} collective-permute-done((f32[256,1024]{0,1:T(8,128)}, f32[256,1024]{0,1:T(8,128)S(1)}, u32[]{:S(2)}, u32[]{:S(2)}) %collective-permute-start) | collective-permute-done | bytes 1048608 | tf_op jit(solution)/shard_map/ppermute | solution.py:218
  577.9 10.7 %broadcast_select_fusion.1 = (f32[256,1024]{0,1:T(8,128)}, f32[256,1024]{0,1:T(8,128)}) fusion(f32[256,1024]{0,1:T(8,128)S(1)} %collective-permute-done, pred[]{:T(512)S(6)} %eq.23, bf16[256,7168]{1,0:T(8,128)(2,1)S(1)} %bitcast.51, bf16[2,7168,1024]{2,1,0:T(8,128)(2,1)} %get-tuple-element.5), kind=kOutput, calls=%fused_computation.23 | convolution fusion | flops 3758358528 | bytes 21495808 | tf_op jit(solution)/shard_map/dot_general | solution.py:220
  588.6 1.5 collective-permute-start.1
  590.8 0.6 exponential_reduce_fusion
  592.1 0.1 add_bitcast_fusion
  592.2 0.6 multiply_reduce_fusion.2
  592.8 0.1 iota_compare_fusion.2
  592.9 1.4 select_add_fusion
  594.3 17.1 %collective-permute-done.1 = f32[256,1024]{0,1:T(8,128)} collective-permute-done((f32[256,1024]{0,1:T(8,128)}, f32[256,1024]{0,1:T(8,128)}, u32[]{:S(2)}, u32[]{:S(2)}) %collective-permute-start.1) | collective-permute-done | bytes 1048608 | tf_op jit(solution)/shard_map/ppermute | solution.py:223
  611.4 1.4 select_add_fusion.1
  612.9 0.0 copy-start
  612.9 1.5 pad_maximum_fusion
  614.4 1.9 copy.20
  616.3 0.4 multiply_reduce_fusion
  616.7 4.9 psum.28
  621.6 1.5 select_reduce_fusion
  623.1 0.1 divide_bitcast_fusion
  623.2 14.2 %all-gather = f32[8,2,2048]{2,1,0:T(2,128)S(1)} all-gather(f32[1,2,2048]{2,1,0:T(2,128)S(1)} %divide_bitcast_fusion), channel_id=1, replica_groups=mesh['groups'=2,'dp'=4,'mp'=2,'seq'=2] {'dp','seq'}, dimensions={0}, use_global_device_ids=true | all-gather | bytes 147456 | tf_op jit(solution)/shard_map/all_gather | solution.py:261
  637.4 0.1 reshape.85
  637.5 0.4 multiply_reduce_fusion.1
  637.9 0.2 fusion.20
  638.1 5.6 all-reduce
  644.4 0.7 exponential_reduce_fusion.1
  645.8 0.6 multiply_reduce_fusion.3
  (20 shorter events, 0.0 us)
Async XLA Ops:
  532.5 26.2 %collective-permute-start.2 = (f32[256,1024]{0,1:T(8,128)S(1)}, f32[256,1024]{0,1:T(8,128)S(1)}, u32[]{:S(2)}, u32[]{:S(2)}) collective-permute-start(f32[256,1024]{0,1:T(8,128)S(1)} %fusion), channel_id=1, source_target_pairs={{0,4},{4,0},{8,12},{12,8},{1,5},{5,1},{9,13},{13,9},{2,6},{6,2},{1... | collective-permute-start | bytes 3145736 | tf_op jit(solution)/shard_map/ppermute | solution.py:218
  545.6 32.3 %collective-permute-start = (f32[256,1024]{0,1:T(8,128)}, f32[256,1024]{0,1:T(8,128)S(1)}, u32[]{:S(2)}, u32[]{:S(2)}) collective-permute-start(f32[256,1024]{0,1:T(8,128)} %fusion.4), channel_id=1, source_target_pairs={{0,4},{4,0},{8,12},{12,8},{1,5},{5,1},{9,13},{13,9},{2,6},{6,2},{1... | collective-permute-start | bytes 3145736 | tf_op jit(solution)/shard_map/ppermute | solution.py:218
  547.6 30.3 %copy-start.1 = (bf16[2,128,7168]{2,1,0:T(8,128)(2,1)S(1)}, bf16[2,128,7168]{2,1,0:T(8,128)(2,1)}, u32[]{:S(2)}) copy-start(bf16[2,128,7168]{2,1,0:T(8,128)(2,1)} %param.9) | copy-start | bytes 11010052
  569.8 20.9 %copy-start.6 = (s32[1,32]{1,0:T(1,128)S(1)}, s32[1,32]{1,0:T(1,128)}, u32[]{:S(2)}) copy-start(s32[1,32]{1,0:T(1,128)} %param.17) | copy-start | bytes 388
  569.8 22.3 %copy-start.8 = (s32[2]{0:T(128)S(1)}, s32[2]{0:T(128)}, u32[]{:S(2)}) copy-start(s32[2]{0:T(128)} %param.13) | copy-start | bytes 28
  569.8 22.3 %copy-start.7 = (s32[1,31]{1,0:T(1,128)S(1)}, s32[1,31]{1,0:T(1,128)}, u32[]{:S(2)}) copy-start(s32[1,31]{1,0:T(1,128)} %param.16) | copy-start | bytes 376
  569.8 22.4 %copy-start.3 = (bf16[1,2048]{1,0:T(2,128)(2,1)S(1)}, bf16[1,2048]{1,0:T(2,128)(2,1)}, u32[]{:S(2)}) copy-start(bf16[1,2048]{1,0:T(2,128)(2,1)} %param.14) | copy-start | bytes 12292
  569.8 23.1 %collective-permute-start.3 = (f32[256,1024]{0,1:T(8,128)}, f32[256,1024]{0,1:T(8,128)}, u32[]{:S(2)}, u32[]{:S(2)}) collective-permute-start(f32[256,1024]{0,1:T(8,128)} %get-tuple-element.16), channel_id=1, source_target_pairs={{0,2},{2,0},{1,3},{3,1},{4,6},{6,4},{5,7},{7,5},{8,10},{10,8},{9,1... | collective-permute-start | bytes 3145736 | tf_op jit(solution)/shard_map/ppermute | solution.py:223
  588.6 22.8 %collective-permute-start.1 = (f32[256,1024]{0,1:T(8,128)}, f32[256,1024]{0,1:T(8,128)}, u32[]{:S(2)}, u32[]{:S(2)}) collective-permute-start(f32[256,1024]{0,1:T(8,128)} %get-tuple-element.18), channel_id=1, source_target_pairs={{0,2},{2,0},{1,3},{3,1},{4,6},{6,4},{5,7},{7,5},{8,10},{10,8},{9,1... | collective-permute-start | bytes 3145736 | tf_op jit(solution)/shard_map/ppermute | solution.py:223
  592.1 19.4 %copy-start.2 = (f32[256,1024]{0,1:T(8,128)S(1)}, f32[256,1024]{0,1:T(8,128)}, u32[]{:S(2)}) copy-start(f32[256,1024]{0,1:T(8,128)} %get-tuple-element.19) | copy-start | bytes 3145732
  612.9 3.4 copy-start
  614.4 7.3 %copy-start.4 = (f32[2048]{0:T(1024)S(1)}, f32[2048]{0:T(1024)}, u32[]{:S(2)}) copy-start(f32[2048]{0:T(1024)} %param.12) | copy-start | bytes 24580
  645.1 2.0 copy-start.5

commit v3 on v2

--- a/solution.py
+++ b/solution.py
@@ -31,7 +31,7 @@
     return functools.reduce(jnp.logical_and, terms)
 
 
-def gather_kernel(w_ref, h_ref, o_ref, p_ref, t_ref, own_sem, h_send, h_recv, send, recv):
+def gather_kernel(w_ref, h_ref, o_ref, p_ref, t_ref, own_send, own_recv, h_send, h_recv, send, recv):
     z = lax.axis_index("dp")
     y = lax.axis_index("groups")
     c = lax.axis_index("seq")
@@ -135,7 +135,14 @@
         device_id_type=MESH,
     )
     outer = jnp.logical_or(z == 0, z == 3)
-    keep = pltpu.make_async_copy(w_ref, o_ref.at[z % 2], own_sem)
+    keep = pltpu.make_async_remote_copy(
+        src_ref=w_ref,
+        dst_ref=o_ref.at[z % 2],
+        send_sem=own_send,
+        recv_sem=own_recv,
+        device_id=to[CORE],
+        device_id_type=MESH,
+    )
 
     def step(t, carry):
         stream(RIGHT, t)
@@ -196,6 +203,7 @@
             pltpu.SemaphoreType.DMA,
             pltpu.SemaphoreType.DMA,
             pltpu.SemaphoreType.DMA,
+            pltpu.SemaphoreType.DMA,
             pltpu.SemaphoreType.DMA((5, 3, CHUNKS)),
             pltpu.SemaphoreType.DMA((5, 3, CHUNKS)),
         ],
@@ -213,13 +221,16 @@
     swap_pair = [(z, z + 1 - 2 * (z % 2)) for z in range(4)]
     sums = []
     back = []
+    owns = []
     for s in range(2):
         away = jnp.dot(theirs, blocks[s], preferred_element_type=jnp.float32)
         back.append(lax.ppermute(away, "dp", swap_pair))
     for s in range(2):
         own = jnp.dot(flattened, blocks[s], preferred_element_type=jnp.float32)
-        leaves = jnp.where(kept_here, back[s], own)
-        stays = jnp.where(kept_here, own, back[s])
+        owns.append(lax.optimization_barrier(own))
+    for s in range(2):
+        leaves = jnp.where(kept_here, back[s], owns[s])
+        stays = jnp.where(kept_here, owns[s], back[s])
         sums.append(stays + lax.ppermute(leaves, "mp", [(0, 1), (1, 0)]))
     return jnp.concatenate(sums, axis=1)
 

time: 649 us -> 360 us (0.55)
  Pallas kernels: 522 us -> 167 us
  starting transfers between devices: 5.13 us -> 73.2 us
    pallas_call x1, Pallas kernels: 522 us -> 167 us  [gather(): pl.pallas_call(gather_kernel, out_shape=(jax.ShapeDtypeStruct((2, depth,...]
    ppermute x2, starting transfers between devices: 2.08 us -> 70.2 us  [paired_branch(): back.append(lax.ppermute(away, 'dp', swap_pair))]
  transfers between devices with their start and end apart: 4 -> 4, of which waited for: 3 -> 3; matrix products, arithmetic and copies ran while one was open for 6% -> 10% of each run, Pallas kernels for 0% -> 0%
where the time goes in v3:
time: 360 us
  Pallas kernels  167 us (46%)
  starting transfers between devices  73.2 us (20%)
  matrix products  43.6 us (12%)
  waiting for transfers between devices  33.3 us (9%)
  blocking collectives  24.5 us (7%)
  other arithmetic  11.3 us (3%)
  between operations  5.36 us (1%)
    pallas_call x1, Pallas kernels, gather(): pl.pallas_call(gather_kernel, out_shape=(jax.ShapeDtypeStruct((2, depth,...  167 us
    ppermute x2, starting transfers between devices, paired_branch(): back.append(lax.ppermute(away, 'dp', swap_pair))  70.2 us
    dot_general x2, matrix products, paired_branch(): away = jnp.dot(theirs, blocks[s], preferred_element_type=jnp.float32)  26.1 us
    ppermute x2, waiting for transfers between devices, paired_branch(): sums.append(stays + lax.ppermute(leaves, 'mp', [(0, 1), (1, 0)]))  19.6 us
    dot_general x2, matrix products, paired_branch(): own = jnp.dot(flattened, blocks[s], preferred_element_type=jnp.float32)  16.9 us
    all_gather x1, blocking collectives, local(): lax.all_gather(pooled_share, ('dp', 'seq'), axis=0, tiled=True)  14 us
    ppermute x2, waiting for transfers between devices, paired_branch(): back.append(lax.ppermute(away, 'dp', swap_pair))  13.6 us
  transfers between devices with their start and end apart: 4, of which 3 were waited for; matrix products, arithmetic and copies ran while one was open for 10% of the time, Pallas kernels for 0%

profile of v3, /device:TPU:0, one launch (start us, length us, event | category | flops | bytes accessed | tf_op | source)
XLA Modules:
  0.0 359.8 jit_solution(2369634142474615789)
XLA Ops:
  0.6 166.5 %shard_map.112 = (bf16[2,7168,1024]{2,1,0:T(8,128)(2,1)}, bf16[1792,1024]{1,0:T(8,128)(2,1)}, bf16[256,7168]{1,0:T(8,128)(2,1)}) custom-call(bf16[7168,1024]{1,0:T(8,128)(2,1)} %w_ref.1, bf16[256,7168]{1,0:T(8,128)(2,1)} %bitcast.45), custom_call_target="tpu_custom_call" | custom-call | bytes 117440512 | tf_op jit(solution)/shard_map/pallas_call | solution.py:193
  167.2 13.1 %fusion.4 = f32[256,1024]{0,1:T(8,128)} fusion(bf16[256,7168]{1,0:T(8,128)(2,1)} %get-tuple-element.6, bf16[2,7168,1024]{2,1,0:T(8,128)(2,1)} %get-tuple-element.5), kind=kOutput, calls=%fused_computation.4 | convolution fusion | flops 3758096384 | bytes 19398656 | tf_op jit(solution)/shard_map/dot_general | solution.py:226
  180.2 70.2 %collective-permute-start = (f32[256,1024]{0,1:T(8,128)}, f32[256,1024]{0,1:T(8,128)S(1)}, u32[]{:S(2)}, u32[]{:S(2)}) collective-permute-start(f32[256,1024]{0,1:T(8,128)} %fusion.4), channel_id=1, source_target_pairs={{0,4},{4,0},{8,12},{12,8},{1,5},{5,1},{9,13},{13,9},{2,6},{6,2},{1... | collective-permute-start | bytes 3145736 | tf_op jit(solution)/shard_map/ppermute | solution.py:227
  250.4 13.0 %fusion = f32[256,1024]{0,1:T(8,128)} fusion(bf16[256,7168]{1,0:T(8,128)(2,1)} %get-tuple-element.6, bf16[2,7168,1024]{2,1,0:T(8,128)(2,1)} %get-tuple-element.5), kind=kOutput, calls=%fused_computation | convolution fusion | flops 3758096384 | bytes 19398656 | tf_op jit(solution)/shard_map/dot_general | solution.py:226
  263.4 8.5 %fusion.13 = f32[256,1024]{0,1:T(8,128)S(1)} fusion(bf16[256,7168]{1,0:T(8,128)(2,1)} %bitcast.46, bf16[2,7168,1024]{2,1,0:T(8,128)(2,1)} %get-tuple-element.5), kind=kOutput, calls=%fused_computation.18 | convolution fusion | flops 3758096384 | bytes 19398656 | tf_op jit(solution)/shard_map/dot_general | solution.py:229
  272.0 2.6 collective-permute-done
  274.6 1.2 broadcast_select_fusion.1
  275.8 1.6 collective-permute-start.1
  277.3 8.4 %fusion.16 = f32[256,1024]{0,1:T(8,128)S(1)} fusion(bf16[256,7168]{1,0:T(8,128)(2,1)} %bitcast.47, bf16[2,7168,1024]{2,1,0:T(8,128)(2,1)} %get-tuple-element.5), kind=kOutput, calls=%fused_computation.19 | convolution fusion | flops 3758096384 | bytes 19398656 | tf_op jit(solution)/shard_map/dot_general | solution.py:229
  285.8 11.0 %collective-permute-done.2 = f32[256,1024]{0,1:T(8,128)S(1)} collective-permute-done((f32[256,1024]{0,1:T(8,128)}, f32[256,1024]{0,1:T(8,128)S(1)}, u32[]{:S(2)}, u32[]{:S(2)}) %collective-permute-start.2) | collective-permute-done | bytes 1048608 | tf_op jit(solution)/shard_map/ppermute | solution.py:227
  296.8 1.1 broadcast_select_fusion
  297.9 1.5 collective-permute-start.3
  300.0 0.6 exponential_reduce_fusion
  301.4 0.1 add_bitcast_fusion
  301.4 0.6 multiply_reduce_fusion.2
  302.1 0.1 iota_compare_fusion.2
  302.1 1.4 select_add_fusion.1
  303.6 19.6 %collective-permute-done.3 = f32[256,1024]{0,1:T(8,128)} collective-permute-done((f32[256,1024]{0,1:T(8,128)}, f32[256,1024]{0,1:T(8,128)}, u32[]{:S(2)}, u32[]{:S(2)}) %collective-permute-start.3) | collective-permute-done | bytes 1048608 | tf_op jit(solution)/shard_map/ppermute | solution.py:234
  323.2 1.4 select_add_fusion
  324.6 1.5 pad_maximum_fusion
  326.1 1.9 copy.20
  328.1 0.4 multiply_reduce_fusion
  328.5 4.9 %psum.28 = f32[2,128]{1,0:T(2,128)S(1)} all-reduce(f32[2,128]{1,0:T(2,128)S(1)} %multiply_reduce_fusion), channel_id=1, replica_groups=mesh['groups'=2,'dp'=4,'mp'=2,'seq'=2] {'mp'}, use_global_device_ids=true, to_apply=%region_1.2 | all-reduce | flops 256 | bytes 2048 | tf_op jit(solution)/shard_map/psum | solution.py:263
  333.4 1.5 select_reduce_fusion
  334.9 0.1 divide_bitcast_fusion
  335.0 14.0 %all-gather = f32[8,2,2048]{2,1,0:T(2,128)S(1)} all-gather(f32[1,2,2048]{2,1,0:T(2,128)S(1)} %divide_bitcast_fusion), channel_id=1, replica_groups=mesh['groups'=2,'dp'=4,'mp'=2,'seq'=2] {'dp','seq'}, dimensions={0}, use_global_device_ids=true | all-gather | bytes 147456 | tf_op jit(solution)/shard_map/all_gather | solution.py:272
  349.0 0.1 reshape.85
  349.0 0.4 multiply_reduce_fusion.1
  349.5 0.2 fusion.20
  349.7 5.6 %all-reduce = (f32[1,32]{1,0:T(1,128)S(1)}, f32[1,32]{1,0:T(1,128)S(1)}, f32[1]{0:T(128)}) all-reduce(f32[1,32]{1,0:T(1,128)S(1)} %bitcast.48, f32[1,32]{1,0:T(1,128)S(1)} %fusion.20, f32[1]{0:T(128)} %bitcast.10), channel_id=1, replica_groups=mesh['groups'=2,'dp'=4,'mp'=2,'seq'=2] {'mp'}, use_global_device_ids=true, to_apply=%region_7.8 | all-reduce | flops 65 | bytes 520 | tf_op jit(solution)/shard_map/psum | solution.py:283
  356.0 0.7 exponential_reduce_fusion.1
  357.4 0.6 multiply_reduce_fusion.3
  (22 shorter events, 0.1 us)
Async XLA Ops:
  180.2 94.4 %collective-permute-start = (f32[256,1024]{0,1:T(8,128)}, f32[256,1024]{0,1:T(8,128)S(1)}, u32[]{:S(2)}, u32[]{:S(2)}) collective-permute-start(f32[256,1024]{0,1:T(8,128)} %fusion.4), channel_id=1, source_target_pairs={{0,4},{4,0},{8,12},{12,8},{1,5},{5,1},{9,13},{13,9},{2,6},{6,2},{1... | collective-permute-start | bytes 3145736 | tf_op jit(solution)/shard_map/ppermute | solution.py:227
  263.4 33.3 %collective-permute-start.2 = (f32[256,1024]{0,1:T(8,128)}, f32[256,1024]{0,1:T(8,128)S(1)}, u32[]{:S(2)}, u32[]{:S(2)}) collective-permute-start(f32[256,1024]{0,1:T(8,128)} %fusion), channel_id=1, source_target_pairs={{0,4},{4,0},{8,12},{12,8},{1,5},{5,1},{9,13},{13,9},{2,6},{6,2},{1... | collective-permute-start | bytes 3145736 | tf_op jit(solution)/shard_map/ppermute | solution.py:227
  275.8 24.2 %copy-start.6 = (s32[1,32]{1,0:T(1,128)S(1)}, s32[1,32]{1,0:T(1,128)}, u32[]{:S(2)}) copy-start(s32[1,32]{1,0:T(1,128)} %param.17) | copy-start | bytes 388
  275.8 25.5 %copy-start.8 = (s32[2]{0:T(128)S(1)}, s32[2]{0:T(128)}, u32[]{:S(2)}) copy-start(s32[2]{0:T(128)} %param.13) | copy-start | bytes 28
  275.8 25.6 %copy-start.7 = (s32[1,31]{1,0:T(1,128)S(1)}, s32[1,31]{1,0:T(1,128)}, u32[]{:S(2)}) copy-start(s32[1,31]{1,0:T(1,128)} %param.16) | copy-start | bytes 376
  275.8 25.6 %copy-start.3 = (bf16[1,2048]{1,0:T(2,128)(2,1)S(1)}, bf16[1,2048]{1,0:T(2,128)(2,1)}, u32[]{:S(2)}) copy-start(bf16[1,2048]{1,0:T(2,128)(2,1)} %param.14) | copy-start | bytes 12292
  275.8 26.3 %collective-permute-start.1 = (f32[256,1024]{0,1:T(8,128)}, f32[256,1024]{0,1:T(8,128)}, u32[]{:S(2)}, u32[]{:S(2)}) collective-permute-start(f32[256,1024]{0,1:T(8,128)} %broadcast_select_fusion.1), channel_id=1, source_target_pairs={{0,2},{2,0},{1,3},{3,1},{4,6},{6,4},{5,7},{7,5},{8,10},{10,8},{9,1... | collective-permute-start | bytes 3145736 | tf_op jit(solution)/shard_map/ppermute | solution.py:234
  285.7 11.0 %copy-start.1 = (f32[256,1024]{0,1:T(8,128)}, f32[256,1024]{0,1:T(8,128)S(1)}, u32[]{:S(2)}) copy-start(f32[256,1024]{0,1:T(8,128)S(1)} %fusion.16) | copy-start | bytes 3145732
  297.9 25.3 %collective-permute-start.3 = (f32[256,1024]{0,1:T(8,128)}, f32[256,1024]{0,1:T(8,128)}, u32[]{:S(2)}, u32[]{:S(2)}) collective-permute-start(f32[256,1024]{0,1:T(8,128)} %broadcast_select_fusion), channel_id=1, source_target_pairs={{0,2},{2,0},{1,3},{3,1},{4,6},{6,4},{5,7},{7,5},{8,10},{10,8},{9,1... | collective-permute-start | bytes 3145736 | tf_op jit(solution)/shard_map/ppermute | solution.py:234
  301.3 21.9 %copy-start.2 = (f32[256,1024]{0,1:T(8,128)S(1)}, f32[256,1024]{0,1:T(8,128)}, u32[]{:S(2)}) copy-start(f32[256,1024]{0,1:T(8,128)} %copy-done.1) | copy-start | bytes 3145732
  324.6 3.4 copy-start
  326.1 7.3 %copy-start.4 = (f32[2048]{0:T(1024)S(1)}, f32[2048]{0:T(1024)}, u32[]{:S(2)}) copy-start(f32[2048]{0:T(1024)} %param.12) | copy-start | bytes 24580
  356.7 2.0 copy-start.5

commit v4 on v3

--- a/solution.py
+++ b/solution.py
@@ -224,11 +224,12 @@
     owns = []
     for s in range(2):
         away = jnp.dot(theirs, blocks[s], preferred_element_type=jnp.float32)
-        back.append(lax.ppermute(away, "dp", swap_pair))
+        for piece in jnp.split(away, 2, axis=1):
+            back.append(lax.ppermute(piece, "dp", swap_pair))
     for s in range(2):
         own = jnp.dot(flattened, blocks[s], preferred_element_type=jnp.float32)
-        owns.append(lax.optimization_barrier(own))
-    for s in range(2):
+        owns.extend(jnp.split(lax.optimization_barrier(own), 2, axis=1))
+    for s in range(4):
         leaves = jnp.where(kept_here, back[s], owns[s])
         stays = jnp.where(kept_here, owns[s], back[s])
         sums.append(stays + lax.ppermute(leaves, "mp", [(0, 1), (1, 0)]))

time: 360 us -> 357 us (level)
  matrix products: 43.6 us -> 38.1 us
  waiting for transfers between devices: 33.3 us -> 28.9 us
  starting transfers between devices: 73.2 us -> 77.3 us
    ppermute x2 -> x4, waiting for transfers between devices: 13.6 us -> 7.2 us  [paired_branch(): back.append(lax.ppermute(piece, 'dp', swap_pair))]
    dot_general x2, matrix products: 26.1 us -> 20.3 us  [paired_branch(): away = jnp.dot(theirs, blocks[s], preferred_element_type=jnp.float32)]
    ppermute x2 -> x4, starting transfers between devices: 70.2 us -> 72.2 us  [paired_branch(): back.append(lax.ppermute(piece, 'dp', swap_pair))]
    ppermute x2 -> x4, waiting for transfers between devices: 19.6 us -> 21.7 us  [paired_branch(): sums.append(stays + lax.ppermute(leaves, 'mp', [(0, 1), (1, 0)]))]
  transfers between devices with their start and end apart: 4 -> 8, of which waited for: 3 -> 5; matrix products, arithmetic and copies ran while one was open for 10% -> 10% of each run, Pallas kernels for 0% -> 0%
where the time goes in v4:
time: 357 us
  Pallas kernels  167 us (47%)
  starting transfers between devices  77.3 us (22%)
  matrix products  38.1 us (11%)
  waiting for transfers between devices  28.9 us (8%)
  blocking collectives  24.5 us (7%)
  other arithmetic  11.9 us (3%)
  between operations  5.25 us (1%)
  local copies, waits for them, and re-layouts  4.71 us (1%)
    pallas_call x1, Pallas kernels, gather(): pl.pallas_call(gather_kernel, out_shape=(jax.ShapeDtypeStruct((2, depth,...  167 us
    ppermute x4, starting transfers between devices, paired_branch(): back.append(lax.ppermute(piece, 'dp', swap_pair))  72.2 us
    ppermute x4, waiting for transfers between devices, paired_branch(): sums.append(stays + lax.ppermute(leaves, 'mp', [(0, 1), (1, 0)]))  21.7 us
    dot_general x2, matrix products, paired_branch(): away = jnp.dot(theirs, blocks[s], preferred_element_type=jnp.float32)  20.3 us
    dot_general x2, matrix products, paired_branch(): own = jnp.dot(flattened, blocks[s], preferred_element_type=jnp.float32)  17.1 us
    all_gather x1, blocking collectives, local(): lax.all_gather(pooled_share, ('dp', 'seq'), axis=0, tiled=True)  14 us
    ppermute x4, waiting for transfers between devices, paired_branch(): back.append(lax.ppermute(piece, 'dp', swap_pair))  7.2 us
  transfers between devices with their start and end apart: 8, of which 5 were waited for; matrix products, arithmetic and copies ran while one was open for 10% of the time, Pallas kernels for 0%

profile of v4, /device:TPU:0, one launch (start us, length us, event | category | flops | bytes accessed | tf_op | source)
XLA Modules:
  0.0 357.1 jit_solution(15562468778156811969)
XLA Ops:
  0.6 166.5 %shard_map.112 = (bf16[2,7168,1024]{2,1,0:T(8,128)(2,1)}, bf16[1792,1024]{1,0:T(8,128)(2,1)}, bf16[256,7168]{1,0:T(8,128)(2,1)}) custom-call(bf16[7168,1024]{1,0:T(8,128)(2,1)} %w_ref.1, bf16[256,7168]{1,0:T(8,128)(2,1)} %bitcast.45), custom_call_target="tpu_custom_call" | custom-call | bytes 117440512 | tf_op jit(solution)/shard_map/pallas_call | solution.py:193
  167.2 10.2 %fusion.4 = f32[256,1024]{0,1:T(8,128)S(1)} fusion(bf16[256,7168]{1,0:T(8,128)(2,1)} %get-tuple-element.6, bf16[2,7168,1024]{2,1,0:T(8,128)(2,1)} %get-tuple-element.5), kind=kOutput, calls=%fused_computation.4 | convolution fusion | flops 3758096384 | bytes 19398656 | tf_op jit(solution)/shard_map/dot_general | solution.py:226
  177.4 0.9 fusion.23
  178.3 70.2 %collective-permute-start = (f32[256,512]{0,1:T(8,128)S(1)}, f32[256,512]{0,1:T(8,128)S(1)}, u32[]{:S(2)}, u32[]{:S(2)}) collective-permute-start(f32[256,512]{0,1:T(8,128)S(1)} %get-tuple-element.18), channel_id=1, source_target_pairs={{0,4},{4,0},{8,12},{12,8},{1,5},{5,1},{9,13},{13,9},{2,6},{6,2},{1... | collective-permute-start | bytes 1572872 | tf_op jit(solution)/shard_map/ppermute | solution.py:228
  248.4 10.1 %fusion = f32[256,1024]{0,1:T(8,128)S(1)} fusion(bf16[256,7168]{1,0:T(8,128)(2,1)} %get-tuple-element.6, bf16[2,7168,1024]{2,1,0:T(8,128)(2,1)} %get-tuple-element.5), kind=kOutput, calls=%fused_computation | convolution fusion | flops 3758096384 | bytes 19398656 | tf_op jit(solution)/shard_map/dot_general | solution.py:226
  258.6 1.1 fusion.24
  259.7 2.0 collective-permute-start.4
  261.7 8.5 %fusion.13 = f32[256,1024]{0,1:T(8,128)S(1)} fusion(bf16[256,7168]{1,0:T(8,128)(2,1)} %bitcast.46, bf16[2,7168,1024]{2,1,0:T(8,128)(2,1)} %get-tuple-element.5), kind=kOutput, calls=%fused_computation.18 | convolution fusion | flops 3758096384 | bytes 19398656 | tf_op jit(solution)/shard_map/dot_general | solution.py:230
  270.3 0.7 copy-done.1
  271.0 1.5 collective-permute-start.1
  272.5 8.6 %fusion.16 = f32[256,1024]{0,1:T(8,128)S(1)} fusion(bf16[256,7168]{1,0:T(8,128)(2,1)} %bitcast.47, bf16[2,7168,1024]{2,1,0:T(8,128)(2,1)} %get-tuple-element.5), kind=kOutput, calls=%fused_computation.19 | convolution fusion | flops 3758096384 | bytes 19398656 | tf_op jit(solution)/shard_map/dot_general | solution.py:230
  281.8 2.0 collective-permute-done.4
  283.8 1.1 slice_select_fusion.1
  286.0 0.6 multiply_reduce_fusion.2
  286.6 1.1 select_add_fusion.3
  287.8 1.6 collective-permute-start.3
  289.4 5.2 %collective-permute-done.6 = f32[256,512]{0,1:T(8,128)S(1)} collective-permute-done((f32[256,512]{0,1:T(8,128)}, f32[256,512]{0,1:T(8,128)S(1)}, u32[]{:S(2)}, u32[]{:S(2)}) %collective-permute-start.6) | collective-permute-done | bytes 524320 | tf_op jit(solution)/shard_map/ppermute | solution.py:228
  294.6 5.2 %collective-permute-done.5 = f32[256,512]{0,1:T(8,128)S(1)} collective-permute-done((f32[256,512]{0,1:T(8,128)S(1)}, f32[256,512]{0,1:T(8,128)S(1)}, u32[]{:S(2)}, u32[]{:S(2)}) %collective-permute-start.5) | collective-permute-done | bytes 524320 | tf_op jit(solution)/shard_map/ppermute | solution.py:235
  299.8 1.1 select_add_fusion.1
  300.9 1.5 collective-permute-start.7
  303.2 7.9 %collective-permute-done.3 = f32[256,512]{0,1:T(8,128)} collective-permute-done((f32[256,512]{0,1:T(8,128)}, f32[256,512]{0,1:T(8,128)}, u32[]{:S(2)}, u32[]{:S(2)}) %collective-permute-start.3) | collective-permute-done | bytes 524320 | tf_op jit(solution)/shard_map/ppermute | solution.py:235
  311.1 1.1 select_add_fusion.2
  312.3 8.5 %collective-permute-done.7 = f32[256,512]{0,1:T(8,128)} collective-permute-done((f32[256,512]{0,1:T(8,128)}, f32[256,512]{0,1:T(8,128)}, u32[]{:S(2)}, u32[]{:S(2)}) %collective-permute-start.7) | collective-permute-done | bytes 524320 | tf_op jit(solution)/shard_map/ppermute | solution.py:235
  320.8 1.1 select_add_fusion
  322.0 1.5 pad_maximum_fusion
  323.5 1.9 copy.24
  325.8 4.9 %psum.28 = f32[2,128]{1,0:T(2,128)S(1)} all-reduce(f32[2,128]{1,0:T(2,128)S(1)} %multiply_reduce_fusion), channel_id=1, replica_groups=mesh['groups'=2,'dp'=4,'mp'=2,'seq'=2] {'mp'}, use_global_device_ids=true, to_apply=%region_1.2 | all-reduce | flops 256 | bytes 2048 | tf_op jit(solution)/shard_map/psum | solution.py:264
  330.8 1.5 select_reduce_fusion
  332.3 14.0 %all-gather = f32[8,2,2048]{2,1,0:T(2,128)S(1)} all-gather(f32[1,2,2048]{2,1,0:T(2,128)S(1)} %divide_bitcast_fusion), channel_id=1, replica_groups=mesh['groups'=2,'dp'=4,'mp'=2,'seq'=2] {'dp','seq'}, dimensions={0}, use_global_device_ids=true | all-gather | bytes 147456 | tf_op jit(solution)/shard_map/all_gather | solution.py:273
  347.0 5.6 %all-reduce = (f32[1,32]{1,0:T(1,128)S(1)}, f32[1,32]{1,0:T(1,128)S(1)}, f32[1]{0:T(128)}) all-reduce(f32[1,32]{1,0:T(1,128)S(1)} %bitcast.48, f32[1,32]{1,0:T(1,128)S(1)} %fusion.20, f32[1]{0:T(128)} %bitcast.10), channel_id=1, replica_groups=mesh['groups'=2,'dp'=4,'mp'=2,'seq'=2] {'mp'}, use_global_device_ids=true, to_apply=%region_7.8 | all-reduce | flops 65 | bytes 520 | tf_op jit(solution)/shard_map/psum | solution.py:284
  353.3 0.7 exponential_reduce_fusion.1
  354.7 0.6 multiply_reduce_fusion.3
  (38 shorter events, 2.6 us)
Async XLA Ops:
  178.3 92.0 %collective-permute-start = (f32[256,512]{0,1:T(8,128)S(1)}, f32[256,512]{0,1:T(8,128)S(1)}, u32[]{:S(2)}, u32[]{:S(2)}) collective-permute-start(f32[256,512]{0,1:T(8,128)S(1)} %get-tuple-element.18), channel_id=1, source_target_pairs={{0,4},{4,0},{8,12},{12,8},{1,5},{5,1},{9,13},{13,9},{2,6},{6,2},{1... | collective-permute-start | bytes 1572872 | tf_op jit(solution)/shard_map/ppermute | solution.py:228
  248.4 38.2 %collective-permute-start.2 = (f32[256,512]{0,1:T(8,128)}, f32[256,512]{0,1:T(8,128)S(1)}, u32[]{:S(2)}, u32[]{:S(2)}) collective-permute-start(f32[256,512]{0,1:T(8,128)} %get-tuple-element.19), channel_id=1, source_target_pairs={{0,4},{4,0},{8,12},{12,8},{1,5},{5,1},{9,13},{13,9},{2,6},{6,2},{1... | collective-permute-start | bytes 1572872 | tf_op jit(solution)/shard_map/ppermute | solution.py:228
  259.7 24.1 %collective-permute-start.4 = (f32[256,512]{0,1:T(8,128)}, f32[256,512]{0,1:T(8,128)}, u32[]{:S(2)}, u32[]{:S(2)}) collective-permute-start(f32[256,512]{0,1:T(8,128)} %get-tuple-element.22), channel_id=1, source_target_pairs={{0,4},{4,0},{8,12},{12,8},{1,5},{5,1},{9,13},{13,9},{2,6},{6,2},{1... | collective-permute-start | bytes 1572872 | tf_op jit(solution)/shard_map/ppermute | solution.py:228
  261.7 32.9 %collective-permute-start.6 = (f32[256,512]{0,1:T(8,128)}, f32[256,512]{0,1:T(8,128)S(1)}, u32[]{:S(2)}, u32[]{:S(2)}) collective-permute-start(f32[256,512]{0,1:T(8,128)} %get-tuple-element.23), channel_id=1, source_target_pairs={{0,4},{4,0},{8,12},{12,8},{1,5},{5,1},{9,13},{13,9},{2,6},{6,2},{1... | collective-permute-start | bytes 1572872 | tf_op jit(solution)/shard_map/ppermute | solution.py:228
  270.2 0.8 copy-start.1
  271.0 14.4 %copy-start.8 = (s32[1,32]{1,0:T(1,128)S(1)}, s32[1,32]{1,0:T(1,128)}, u32[]{:S(2)}) copy-start(s32[1,32]{1,0:T(1,128)} %param.17) | copy-start | bytes 388
  271.0 15.0 %copy-start.5 = (bf16[1,2048]{1,0:T(2,128)(2,1)S(1)}, bf16[1,2048]{1,0:T(2,128)(2,1)}, u32[]{:S(2)}) copy-start(bf16[1,2048]{1,0:T(2,128)(2,1)} %param.14) | copy-start | bytes 12292
  271.0 15.6 %collective-permute-start.1 = (f32[256,512]{0,1:T(8,128)S(1)}, f32[256,512]{0,1:T(8,128)S(1)}, u32[]{:S(2)}, u32[]{:S(2)}) collective-permute-start(f32[256,512]{0,1:T(8,128)S(1)} %slice_select_fusion.3), channel_id=1, source_target_pairs={{0,2},{2,0},{1,3},{3,1},{4,6},{6,4},{5,7},{7,5},{8,10},{10,8},{9,1... | collective-permute-start | bytes 1572872 | tf_op jit(solution)/shard_map/ppermute | solution.py:235
  272.5 14.1 %copy-start.2 = (f32[256,512]{0,1:T(8,128)S(1)}, f32[256,512]{0,1:T(8,128)}, u32[]{:S(2)}) copy-start(f32[256,512]{0,1:T(8,128)} %copy-done.1) | copy-start | bytes 1572868
  284.9 14.9 %collective-permute-start.5 = (f32[256,512]{0,1:T(8,128)S(1)}, f32[256,512]{0,1:T(8,128)S(1)}, u32[]{:S(2)}, u32[]{:S(2)}) collective-permute-start(f32[256,512]{0,1:T(8,128)S(1)} %slice_select_fusion.1), channel_id=1, source_target_pairs={{0,2},{2,0},{1,3},{3,1},{4,6},{6,4},{5,7},{7,5},{8,10},{10,8},{9,1... | collective-permute-start | bytes 1572872 | tf_op jit(solution)/shard_map/ppermute | solution.py:235
  286.6 15.8 %copy-start.9 = (s32[1,31]{1,0:T(1,128)S(1)}, s32[1,31]{1,0:T(1,128)}, u32[]{:S(2)}) copy-start(s32[1,31]{1,0:T(1,128)} %param.16) | copy-start | bytes 376
  286.6 15.9 %copy-start.10 = (s32[2]{0:T(128)S(1)}, s32[2]{0:T(128)}, u32[]{:S(2)}) copy-start(s32[2]{0:T(128)} %param.13) | copy-start | bytes 28
  287.8 23.4 %collective-permute-start.3 = (f32[256,512]{0,1:T(8,128)}, f32[256,512]{0,1:T(8,128)}, u32[]{:S(2)}, u32[]{:S(2)}) collective-permute-start(f32[256,512]{0,1:T(8,128)} %get-tuple-element.17), channel_id=1, source_target_pairs={{0,2},{2,0},{1,3},{3,1},{4,6},{6,4},{5,7},{7,5},{8,10},{10,8},{9,1... | collective-permute-start | bytes 1572872 | tf_op jit(solution)/shard_map/ppermute | solution.py:235
  300.9 19.9 %collective-permute-start.7 = (f32[256,512]{0,1:T(8,128)}, f32[256,512]{0,1:T(8,128)}, u32[]{:S(2)}, u32[]{:S(2)}) collective-permute-start(f32[256,512]{0,1:T(8,128)} %get-tuple-element.21), channel_id=1, source_target_pairs={{0,2},{2,0},{1,3},{3,1},{4,6},{6,4},{5,7},{7,5},{8,10},{10,8},{9,1... | collective-permute-start | bytes 1572872 | tf_op jit(solution)/shard_map/ppermute | solution.py:235
  303.1 18.8 %copy-start.3 = (f32[256,512]{0,1:T(8,128)S(1)}, f32[256,512]{0,1:T(8,128)}, u32[]{:S(2)}) copy-start(f32[256,512]{0,1:T(8,128)} %get-tuple-element.16) | copy-start | bytes 1572868
  303.1 18.8 %copy-start.4 = (f32[256,512]{0,1:T(8,128)S(1)}, f32[256,512]{0,1:T(8,128)}, u32[]{:S(2)}) copy-start(f32[256,512]{0,1:T(8,128)} %get-tuple-element.20) | copy-start | bytes 1572868
  322.0 3.4 copy-start
  323.5 7.3 %copy-start.6 = (f32[2048]{0:T(1024)S(1)}, f32[2048]{0:T(1024)}, u32[]{:S(2)}) copy-start(f32[2048]{0:T(1024)} %param.12) | copy-start | bytes 24580
  354.0 2.0 copy-start.7
